TPU v7x, 32 devices: a whole 2x2x4 slice. The times are simulated.
32 devices in a mesh: sec: 2 (over core), ctx: 8 (over z, x), head: 2 (over y).
Axes of the slice: x: 2, y: 2, z: 4, core: 2. Of those that a mesh axis runs over, the one named last changes fastest.
Arguments:
- query_self: bfloat16 [1536, 2048], P('ctx', ('sec', 'head')), may hold values from -12 to 12
- key_self: bfloat16 [1536, 2048], P('ctx', ('sec', 'head')), may hold values from -6 to 6
- value_self: bfloat16 [1536, 2048], P('ctx', ('sec', 'head')), may hold values from -6 to 6
- query_cross: bfloat16 [1536, 2048], P('ctx', ('sec', 'head')), may hold values from -12 to 12
- neighbour_kv: bfloat16 [32, 128, 4096], P(('sec', 'ctx', 'head')), may hold values from -6 to 6
- neighbour_map: int32 [24, 2], P('ctx'), may hold values from 0 to 3, all different within a row
Outputs:
- self_out: bfloat16 [1536, 2048], P('ctx', ('sec', 'head'))
- cross_out: bfloat16 [1536, 2048], P('ctx', ('sec', 'head'))
Inputs may be any that keep to these rules, and one draw needn't show every extreme that they name: `neighbour_map`: entry v of stretch c names slot v % 1 of the device at index v // 1 along sec+head that shares stretch c's context shard; a stretch's two entries differ.
All inputs are finite; a program needn't handle non-finite values.
Results may differ from a plain program's by a relative error of at most 0.0035.
Values may be sent and summed in bfloat16 or wider, within the bound.
A program may use at most 64 MiB of HBM per device.

v0:
```python
import math

import jax
import jax.numpy as jnp
from jax import lax
from jax.sharding import PartitionSpec as P

HD = 128
STRETCH = 64


MASKED_SCORE = -1e30


def from_behind(value, axis, steps):
    count = lax.axis_size(axis)
    leading, last = (max(0, -steps), min(count, count - steps))
    return lax.ppermute(value, axis, [(source, source + steps) for source in range(leading, last)])


def attend_block(carried, queries, key_block, value_block, key_mask, score_scale):
    row_top, row_total, summed = carried
    scores = (
        jnp.einsum("qhd,khd->hqk", queries, key_block, preferred_element_type=jnp.float32)
        * score_scale
    )
    masked = jnp.where(key_mask, scores, MASKED_SCORE)
    new_top = jnp.maximum(row_top, jnp.max(masked, axis=-1))
    exp_scores = jnp.where(key_mask, jnp.exp(masked - new_top[:, :, None]), 0.0)
    factor = jnp.exp(row_top - new_top)
    row_total = row_total * factor + jnp.sum(exp_scores, axis=-1)
    update = jnp.einsum(
        "hqk,khd->qhd",
        exp_scores.astype(jnp.bfloat16),
        value_block,
        preferred_element_type=jnp.float32,
    )
    summed = summed * jnp.transpose(factor)[:, :, None] + update
    return (new_top, row_total, summed)


def attend_keys(carried, queries, key_rows, value_rows, first_row, positions, score_scale):
    key_count = key_rows.shape[0]
    head_count = queries.shape[1]
    block_rows = key_count if key_count <= 1024 else math.gcd(key_count, 1024)
    blocks = key_count // block_rows
    key_stack = key_rows.reshape(blocks, block_rows, head_count, HD)
    value_stack = value_rows.reshape(blocks, block_rows, head_count, HD)

    def fold_step(state_now, scanned):
        number, key_block, value_block = scanned
        places = first_row + number * block_rows + jnp.arange(block_rows, dtype=jnp.int32)
        key_mask = (places[None, None, :] <= positions[None, :, None]) & (
            places[None, None, :] >= 0
        )
        return (
            attend_block(state_now, queries, key_block, value_block, key_mask, score_scale),
            None,
        )

    carried, _ = lax.scan(
        fold_step, carried, (jnp.arange(blocks, dtype=jnp.int32), key_stack, value_stack)
    )
    return carried


def self_attention(query_self, key_self, value_self, score_scale):
    local_rows, local_width = query_self.shape
    head_count = local_width // HD
    queries = query_self.reshape(local_rows, head_count, HD)
    first_row = lax.axis_index("ctx") * local_rows
    positions = first_row + jnp.arange(local_rows, dtype=jnp.int32)
    carried = (
        jnp.full((head_count, local_rows), MASKED_SCORE, jnp.float32),
        jnp.zeros((head_count, local_rows), jnp.float32),
        jnp.zeros((local_rows, head_count, HD), jnp.float32),
    )
    carried = attend_keys(carried, queries, key_self, value_self, first_row, positions, score_scale)
    window = jnp.concatenate([key_self, value_self], axis=1)
    distance = 1
    shards = lax.axis_size("ctx")
    while distance < shards:
        arrived = from_behind(window, "ctx", distance)
        carried = attend_keys(
            carried,
            queries,
            arrived[:, :local_width],
            arrived[:, local_width:],
            first_row - (2 * distance - 1) * local_rows,
            positions,
            score_scale,
        )
        if 2 * distance < shards:
            window = jnp.concatenate([arrived, window], axis=0)
        distance = distance * 2
    row_top, row_total, summed = carried
    attended = summed / jnp.transpose(row_total)[:, :, None]
    return attended.reshape(local_rows, local_width).astype(jnp.bfloat16)


def cross_attention(query_cross, neighbour_kv, neighbour_map, score_scale):
    local_rows, local_width = query_cross.shape
    head_count = local_width // HD
    stretch_count = local_rows // STRETCH
    slot_count, block_len, features = neighbour_kv.shape
    group_count = features // (2 * local_width)
    stretch_first = lax.axis_index("ctx") * stretch_count
    keep_stretch = stretch_first + jnp.arange(stretch_count, dtype=jnp.int32) > 0
    parted = neighbour_kv.reshape(slot_count, block_len, group_count, 2 * local_width)
    received = lax.all_to_all(parted, ("sec", "head"), split_axis=2, concat_axis=0, tiled=True)
    received = received.reshape(group_count * slot_count, block_len, 2, head_count, HD)
    chosen = received[neighbour_map]
    chosen = chosen.reshape(stretch_count, neighbour_map.shape[1] * block_len, 2, head_count, HD)
    stretch_queries = query_cross.reshape(stretch_count, STRETCH, head_count, HD)
    scores = (
        jnp.einsum(
            "cqhd,ckhd->chqk", stretch_queries, chosen[:, :, 0], preferred_element_type=jnp.float32
        )
        * score_scale
    )
    row_top = jnp.max(scores, axis=-1, keepdims=True)
    exp_scores = jnp.exp(scores - row_top)
    row_total = jnp.sum(exp_scores, axis=-1)
    summed = jnp.einsum(
        "chqk,ckhd->cqhd",
        exp_scores.astype(jnp.bfloat16),
        chosen[:, :, 1],
        preferred_element_type=jnp.float32,
    )
    attended = summed / jnp.transpose(row_total, (0, 2, 1))[:, :, :, None]
    attended = attended.reshape(local_rows, local_width)
    keep_rows = jnp.repeat(keep_stretch, STRETCH)
    return jnp.where(keep_rows[:, None], attended, 0.0).astype(jnp.bfloat16)


def on_device(query_self, key_self, value_self, query_cross, neighbour_kv, neighbour_map):
    score_scale = 1.0 / math.sqrt(HD)
    self_out = self_attention(query_self, key_self, value_self, score_scale)
    cross_out = cross_attention(query_cross, neighbour_kv, neighbour_map, score_scale)
    return (self_out, cross_out)


def solution(mesh):
    return jax.shard_map(
        on_device,
        mesh=mesh,
        in_specs=(
            P("ctx", ("sec", "head")),
            P("ctx", ("sec", "head")),
            P("ctx", ("sec", "head")),
            P("ctx", ("sec", "head")),
            P(("sec", "ctx", "head"), None, None),
            P("ctx", None),
        ),
        out_specs=(P("ctx", ("sec", "head")), P("ctx", ("sec", "head"))),
        check_vma=False,
    )
```

profile of v0, /device:TPU:25, one launch (start us, length us, event | category | flops | bytes accessed | tf_op | source)
XLA Modules:
  0.0 119.5 jit_solution(18434310506208700679)
XLA Ops:
  0.7 1.2 copy.104
  1.8 1.1 copy.103
  3.0 3.1 %collective-permute-start = (bf16[192,1024]{0,1:T(8,128)(2,1)S(1)}, bf16[192,1024]{0,1:T(8,128)(2,1)S(1)}, u32[]{:S(2)}, u32[]{:S(2)}) collective-permute-start(bf16[192,1024]{0,1:T(8,128)(2,1)S(1)} %pad_maximum_fusion), channel_id=1, source_target_pairs={{0,2},{2,4},{4,6},{6,8},{8,10},{10,12},{12,14},{1,3},{3,5},{5,7},{... | collective-permute-start | bytes 1179656 | tf_op jit(solution)/shard_map/ppermute | solution.py:18
  6.1 1.3 %copy.118 = bf16[1,128,4096]{1,2,0:T(8,128)(2,1)} copy(bf16[1,128,4096]{2,1,0:T(8,128)(2,1)S(1)} %copy-done.2) | data formatting | bytes 2097152 | tf_op args[4]
  7.4 4.6 %all-to-all-start = ((bf16[1,128,4,1024]{1,3,0,2:T(8,128)(2,1)}), bf16[1,128,4,1024]{1,3,0,2:T(8,128)(2,1)S(1)}, u32[]{:S(2)}, u32[]{:S(2)}) async-start(bf16[1,128,4,1024]{1,3,0,2:T(8,128)(2,1)} %bitcast.209), calls=%async_computation | async-start | bytes 2097152 | tf_op jit(solution)/shard_map/all_to_all | solution.py:110
  12.6 0.6 pad_clamp_fusion
  13.4 5.2 %collective-permute-done = bf16[192,1024]{0,1:T(8,128)(2,1)S(1)} collective-permute-done((bf16[192,1024]{0,1:T(8,128)(2,1)S(1)}, bf16[192,1024]{0,1:T(8,128)(2,1)S(1)}, u32[]{:S(2)}, u32[]{:S(2)}) %collective-permute-start) | collective-permute-done | bytes 393248 | tf_op jit(solution)/shard_map/ppermute | solution.py:18
  18.6 1.2 %maximum_maximum_fusion.1 = bf16[384,1024]{0,1:T(8,128)(2,1)} fusion(bf16[192,512]{0,1:T(8,128)(2,1)S(1)} %copy.104, bf16[192,512]{0,1:T(8,128)(2,1)S(1)} %copy.103, bf16[192,1024]{0,1:T(8,128)(2,1)S(1)} %collective-permute-done), kind=kLoop, calls=%fused_computation.40 | loop fusion | flops 2359296 | bytes 1572864 | tf_op jit(solution)/shard_map/concatenate | solution.py:94
  19.8 1.3 %collective-permute-start.1 = (bf16[384,1024]{0,1:T(8,128)(2,1)}, bf16[384,1024]{0,1:T(8,128)(2,1)}, u32[]{:S(2)}, u32[]{:S(2)}) collective-permute-start(bf16[384,1024]{0,1:T(8,128)(2,1)} %maximum_maximum_fusion.1), channel_id=1, source_target_pairs={{0,4},{2,6},{4,8},{6,10},{8,12},{10,14},{1,5},{3,7},{5,9},{7,11},{... | collective-permute-start | bytes 2359304 | tf_op jit(solution)/shard_map/ppermute | solution.py:18
  21.1 1.0 reshape.311
  22.1 0.6 broadcast_in_dim.166
  22.7 1.2 fusion.89
  23.9 0.7 fusion.86
  25.0 0.6 all-to-all-done
  25.6 1.0 copy-done.1
  26.6 1.6 %copy.120 = bf16[4,128,2,4,128]{4,1,3,2,0:T(8,128)(2,1)S(1)} copy(bf16[4,128,2,4,128]{1,4,3,2,0:T(8,128)(2,1)} %bitcast.208) | data formatting | bytes 2097152 | tf_op jit(solution)/shard_map/reshape | solution.py:111
  28.2 2.1 %gather_fusion = bf16[6,128,2,4,128]{4,1,3,2,0:T(8,128)(2,1)} fusion(bf16[4,128,2,4,128]{4,1,3,2,0:T(8,128)(2,1)S(1)} %copy.120, s32[1024]{0:T(1024)} %pad_clamp_fusion), kind=kCustom, calls=%fused_computation | custom fusion | bytes 3145752 | tf_op jit(solution)/shard_map/gather | solution.py:112
  30.3 1.5 %copy.121 = bf16[6,128,2,4,128]{4,1,0,3,2:T(8,128)(2,1)S(1)} copy(bf16[6,128,2,4,128]{4,1,3,2,0:T(8,128)(2,1)} %gather_fusion) | data formatting | bytes 3145728 | tf_op jit(solution)/shard_map/gather | solution.py:112
  31.8 7.6 %collective-permute-done.1 = bf16[384,1024]{0,1:T(8,128)(2,1)} collective-permute-done((bf16[384,1024]{0,1:T(8,128)(2,1)}, bf16[384,1024]{0,1:T(8,128)(2,1)}, u32[]{:S(2)}, u32[]{:S(2)}) %collective-permute-start.1) | collective-permute-done | bytes 786464 | tf_op jit(solution)/shard_map/ppermute | solution.py:18
  39.5 1.5 %maximum_maximum_fusion = bf16[768,1024]{0,1:T(8,128)(2,1)S(1)} fusion(bf16[192,512]{0,1:T(8,128)(2,1)S(1)} %copy.104, bf16[192,512]{0,1:T(8,128)(2,1)S(1)} %copy.103, bf16[192,1024]{0,1:T(8,128)(2,1)S(1)} %collective-permute-done, bf16[384,1024]{0,1:T(8,128)(2,1)} %collective-permute-done.1), kind=kLoop, calls=%fused_computation.6 | loop fusion | flops 6291456 | bytes 3145728 | tf_op jit(solution)/shard_map/concatenate | solution.py:94
  40.9 1.3 %collective-permute-start.2 = (bf16[768,1024]{0,1:T(8,128)(2,1)S(1)}, bf16[768,1024]{0,1:T(8,128)(2,1)S(1)}, u32[]{:S(2)}, u32[]{:S(2)}) collective-permute-start(bf16[768,1024]{0,1:T(8,128)(2,1)S(1)} %maximum_maximum_fusion), channel_id=1, source_target_pairs={{0,8},{2,10},{4,12},{6,14},{1,9},{3,11},{5,13},{7,15},{16,24},{18,... | collective-permute-start | bytes 4718600 | tf_op jit(solution)/shard_map/ppermute | solution.py:18
  42.3 0.5 fusion.90
  43.8 0.8 fusion.44
  44.6 1.2 fusion.85
  46.2 67.4 %collective-permute-done.2 = bf16[768,1024]{0,1:T(8,128)(2,1)S(1)} collective-permute-done((bf16[768,1024]{0,1:T(8,128)(2,1)S(1)}, bf16[768,1024]{0,1:T(8,128)(2,1)S(1)}, u32[]{:S(2)}, u32[]{:S(2)}) %collective-permute-start.2) | collective-permute-done | bytes 1572896 | tf_op jit(solution)/shard_map/ppermute | solution.py:18
  113.7 0.7 fusion
  114.4 0.5 fusion.29
  115.4 0.8 fusion.1
  116.8 0.5 fusion.17
  117.4 0.5 fusion.16
  117.9 0.9 fusion.26
  118.8 0.7 copy.189
  (49 shorter events, 3.9 us)
Async XLA Ops:
  0.6 22.1 %copy-start = (bf16[192,512]{1,0:T(8,128)(2,1)S(1)}, bf16[192,512]{1,0:T(8,128)(2,1)}, u32[]{:S(2)}) copy-start(bf16[192,512]{1,0:T(8,128)(2,1)} %param.6) | copy-start | bytes 589828
  0.6 5.5 %copy-start.2 = (bf16[1,128,4096]{2,1,0:T(8,128)(2,1)S(1)}, bf16[1,128,4096]{2,1,0:T(8,128)(2,1)}, u32[]{:S(2)}) copy-start(bf16[1,128,4096]{2,1,0:T(8,128)(2,1)} %param.10) | copy-start | bytes 3145732
  3.0 15.6 %collective-permute-start = (bf16[192,1024]{0,1:T(8,128)(2,1)S(1)}, bf16[192,1024]{0,1:T(8,128)(2,1)S(1)}, u32[]{:S(2)}, u32[]{:S(2)}) collective-permute-start(bf16[192,1024]{0,1:T(8,128)(2,1)S(1)} %pad_maximum_fusion), channel_id=1, source_target_pairs={{0,2},{2,4},{4,6},{6,8},{8,10},{10,12},{12,14},{1,3},{3,5},{5,7},{... | collective-permute-start | bytes 1179656 | tf_op jit(solution)/shard_map/ppermute | solution.py:18
  7.4 4.7 %copy-start.9 = (s32[3,2]{0,1:T(2,128)S(1)}, s32[3,2]{0,1:T(2,128)}, u32[]{:S(2)}) copy-start(s32[3,2]{0,1:T(2,128)} %param.11) | copy-start | bytes 76
  7.4 18.2 %all-to-all-start = ((bf16[1,128,4,1024]{1,3,0,2:T(8,128)(2,1)}), bf16[1,128,4,1024]{1,3,0,2:T(8,128)(2,1)S(1)}, u32[]{:S(2)}, u32[]{:S(2)}) async-start(bf16[1,128,4,1024]{1,3,0,2:T(8,128)(2,1)} %bitcast.209), calls=%async_computation | async-start | bytes 2097152 | tf_op jit(solution)/shard_map/all_to_all | solution.py:110
  12.0 10.7 %copy-start.7 = (bf16[192,512]{1,0:T(8,128)(2,1)S(1)}, bf16[192,512]{1,0:T(8,128)(2,1)}, u32[]{:S(2)}) copy-start(bf16[192,512]{1,0:T(8,128)(2,1)} %param.7) | copy-start | bytes 589828
  12.4 11.5 %copy-start.5 = (pred[192,192]{0,1:T(8,128)(4,1)}, pred[192,192]{0,1:T(8,128)(4,1)S(1)}, u32[]{:S(2)}) copy-start(pred[192,192]{0,1:T(8,128)(4,1)S(1)} %get-tuple-element.109) | copy-start | bytes 110596
  19.8 19.7 %collective-permute-start.1 = (bf16[384,1024]{0,1:T(8,128)(2,1)}, bf16[384,1024]{0,1:T(8,128)(2,1)}, u32[]{:S(2)}, u32[]{:S(2)}) collective-permute-start(bf16[384,1024]{0,1:T(8,128)(2,1)} %maximum_maximum_fusion.1), channel_id=1, source_target_pairs={{0,4},{2,6},{4,8},{6,10},{8,12},{10,14},{1,5},{3,7},{5,9},{7,11},{... | collective-permute-start | bytes 2359304 | tf_op jit(solution)/shard_map/ppermute | solution.py:18
  25.6 1.0 copy-start.1
  40.9 72.7 %collective-permute-start.2 = (bf16[768,1024]{0,1:T(8,128)(2,1)S(1)}, bf16[768,1024]{0,1:T(8,128)(2,1)S(1)}, u32[]{:S(2)}, u32[]{:S(2)}) collective-permute-start(bf16[768,1024]{0,1:T(8,128)(2,1)S(1)} %maximum_maximum_fusion), channel_id=1, source_target_pairs={{0,8},{2,10},{4,12},{6,14},{1,9},{3,11},{5,13},{7,15},{16,24},{18,... | collective-permute-start | bytes 4718600 | tf_op jit(solution)/shard_map/ppermute | solution.py:18
  43.2 0.6 copy-start.10
  115.3 1.1 copy-start.4
  115.3 1.1 copy-start.6
  115.4 1.5 %copy-start.8 = (bf16[192,512]{1,0:T(8,128)(2,1)S(1)}, bf16[192,512]{1,0:T(8,128)(2,1)}, u32[]{:S(2)}) copy-start(bf16[192,512]{1,0:T(8,128)(2,1)} %param.8) | copy-start | bytes 589828
  116.5 1.0 copy-start.3
where the time goes:
time: 120 us
  waiting for transfers between devices  80.8 us (67%)
  local copies, waits for them, and re-layouts  15.1 us (13%)
  starting transfers between devices  10.3 us (9%)
  other arithmetic  6.71 us (6%)
  matrix products  5.74 us (5%)
    ppermute x3, waiting for transfers between devices, from_behind(): lax.ppermute(value, axis, [(source, source + steps) for source in range(l...  80.2 us
    ppermute x3, starting transfers between devices, from_behind(): lax.ppermute(value, axis, [(source, source + steps) for source in range(l...  5.69 us
    unnamed x25, local copies, waits for them, and re-layouts  5.02 us
    all_to_all x1, starting transfers between devices, cross_attention(): lax.all_to_all(parted, ('sec', 'head'), split_axis=2, concat_axis=0, tile...  4.57 us
    gather x2, local copies, waits for them, and re-layouts, cross_attention(): chosen = received[neighbour_map]  3.59 us
    concatenate x2, other arithmetic, self_attention(): window = jnp.concatenate([arrived, window], axis=0)  2.68 us
    dot_general x4, matrix products, attend_block(): jnp.einsum('qhd,khd->hqk', queries, key_block, preferred_element_type=jnp...  2.64 us
  transfers between devices with their start and end apart: 4, of which 4 were waited for; matrix products, arithmetic and copies ran while one was open for 14% of the time, Pallas kernels for 0%

commit v1 on v0

v1 whole, which is shorter than its diff:
```python
import functools
import math

import jax
import jax.numpy as jnp
from jax import lax
from jax.experimental import pallas as pl
from jax.experimental.pallas import tpu as pltpu
from jax.sharding import PartitionSpec as P

HD = 128
STRETCH = 64
MASKED_SCORE = -1e30
MESH = pl.DeviceIdType.MESH
BASE2 = math.log2(math.e) / math.sqrt(HD)


def scores_of(queries, keys):
    return lax.dot_general(
        queries, keys, (((1,), (1,)), ((), ())), preferred_element_type=jnp.float32
    )


def attend(queries, keys, values, mask=None):
    scores = scores_of(queries, keys)
    if mask is not None:
        scores = jnp.where(mask, scores, MASKED_SCORE)
    top = jnp.max(scores, axis=-1, keepdims=True) * BASE2
    probs = jnp.exp2(scores * BASE2 - top)
    total = jnp.sum(probs, axis=-1, keepdims=True)
    summed = jnp.dot(probs.astype(jnp.bfloat16), values, preferred_element_type=jnp.float32)
    return summed, top, total


def kernel(
    sizes,
    map_ref,
    qs_ref,
    k_ref,
    v_ref,
    qc_ref,
    nb_ref,
    so_ref,
    co_ref,
    k_all,
    v_all,
    q_in,
    o_part,
    l_part,
    o_in,
    l_in,
    own_sum,
    own_top,
    own_total,
    nb_all,
    kv_send,
    kv_recv,
    q_send,
    q_recv,
    o_send,
    o_recv,
    nb_send,
    nb_recv,
    nb_own,
):
    n_sec, n_ctx, n_head = sizes
    half = n_ctx // 2
    rows, width = qs_ref.shape
    heads = width // HD
    group = n_sec * n_head
    slots = nb_ref.shape[0]

    sec, ctx, head = (lax.axis_index(a) for a in ("sec", "ctx", "head"))
    upper = ctx >= half
    mine = lax.rem(ctx, half)
    base = ctx - mine
    partner = lax.rem(ctx + half, n_ctx)
    within = sec * n_head + head

    def member(d):
        other = lax.rem(within + d, group)
        return other, {"sec": other // n_head, "head": lax.rem(other, n_head)}

    def peer(d):
        return base + lax.rem(mine + d, half)

    def cols(h):
        return slice(h * HD, (h + 1) * HD)

    barrier = pltpu.get_barrier_semaphore()
    for d in range(1, half):
        pl.semaphore_signal(barrier, inc=1, device_id={"ctx": peer(d)}, device_id_type=MESH)
    pl.semaphore_signal(barrier, inc=1, device_id={"ctx": partner}, device_id_type=MESH)
    for d in range(1, group):
        pl.semaphore_signal(barrier, inc=1, device_id=member(d)[1], device_id_type=MESH)
    pl.semaphore_wait(barrier, half - 1 + 1 + group - 1)

    def q_copy(h):
        return pltpu.make_async_remote_copy(
            src_ref=qs_ref.at[:, cols(h)],
            dst_ref=q_in.at[:, cols(h)],
            send_sem=q_send.at[h],
            recv_sem=q_recv.at[h],
            device_id={"ctx": partner},
            device_id_type=MESH,
        )

    def kv_copy(d, h, t):
        source, gathered = ((k_ref, k_all), (v_ref, v_all))[t]
        return pltpu.make_async_remote_copy(
            src_ref=source.at[:, cols(h)],
            dst_ref=gathered.at[mine, :, cols(h)],
            send_sem=kv_send.at[d - 1, h, t],
            recv_sem=kv_recv.at[d - 1, h, t],
            device_id={"ctx": peer(d)},
            device_id_type=MESH,
        )

    def o_copy(h, t):
        source, target = ((o_part.at[:, cols(h)], o_in.at[:, cols(h)]), (l_part.at[h], l_in.at[h]))[t]
        return pltpu.make_async_remote_copy(
            src_ref=source,
            dst_ref=target,
            send_sem=o_send.at[h, t],
            recv_sem=o_recv.at[h, t],
            device_id={"ctx": partner},
            device_id_type=MESH,
        )

    def nb_copy(d):
        other, place = member(d)
        start = pl.multiple_of(other * (2 * width), 2 * width)
        return pltpu.make_async_remote_copy(
            src_ref=nb_ref.at[:, :, pl.ds(start, 2 * width)],
            dst_ref=nb_all.at[pl.ds(within * slots, slots)],
            send_sem=nb_send.at[d - 1],
            recv_sem=nb_recv.at[d - 1],
            device_id=place,
            device_id_type=MESH,
        )

    for h in range(heads):
        pl.when(upper)(lambda h=h: q_copy(h).start())
        for d in range(1, half):
            for t in range(2):
                kv_copy(d, h, t).start()
        if h == 0:
            for d in range(1, group):
                nb_copy(d).start()
    own_nb = pltpu.make_async_copy(
        nb_ref.at[:, :, pl.ds(pl.multiple_of(within * (2 * width), 2 * width), 2 * width)],
        nb_all.at[pl.ds(within * slots, slots)],
        nb_own,
    )
    own_nb.start()
    k_all[mine] = k_ref[...]
    v_all[mine] = v_ref[...]

    def gathered_head(h):
        keys = k_all[:, :, cols(h)].reshape(half * rows, HD)
        values = v_all[:, :, cols(h)].reshape(half * rows, HD)
        return keys, values

    def wait_kv(h):
        for d in range(1, half):
            for t in range(2):
                kv_copy(d, h, t).wait_recv()

    def attend_own(h):
        keys, values = gathered_head(h)
        place = lax.broadcasted_iota(jnp.int32, (rows, half * rows), 1)
        position = lax.broadcasted_iota(jnp.int32, (rows, half * rows), 0) + mine * rows
        return attend(qs_ref[:, cols(h)], keys, values, place <= position)

    def cross():
        own_nb.wait()
        for d in range(1, group):
            nb_copy(d).wait_recv()
        for c in range(rows // STRETCH):
            picks = [map_ref[c, r] for r in range(map_ref.shape[1])]
            part = slice(c * STRETCH, (c + 1) * STRETCH)
            keep = jnp.logical_or(ctx > 0, c > 0)
            for h in range(heads):
                keys = jnp.concatenate([nb_all[v, :, cols(h)] for v in picks], axis=0)
                values = jnp.concatenate([nb_all[v, :, cols(heads + h)] for v in picks], axis=0)
                summed, _, total = attend(qc_ref[part, cols(h)], keys, values)
                co_ref[part, cols(h)] = jnp.where(keep, summed / total, 0.0).astype(co_ref.dtype)

    @pl.when(jnp.logical_not(upper))
    def _():
        for h in range(heads):
            wait_kv(h)
            q_copy(h).wait_recv()
            keys, values = gathered_head(h)
            summed, top, total = attend(q_in[:, cols(h)], keys, values)
            o_part[:, cols(h)] = (summed / total).astype(o_part.dtype)
            level = jnp.broadcast_to(top + jnp.log2(total), (rows, HD))
            l_part[h] = jnp.transpose(level)[:8]
            for t in range(2):
                o_copy(h, t).start()
            summed, _, total = attend_own(h)
            so_ref[:, cols(h)] = (summed / total).astype(so_ref.dtype)
        cross()
        for h in range(heads):
            for t in range(2):
                o_copy(h, t).wait_send()

    @pl.when(upper)
    def _():
        for h in range(heads):
            wait_kv(h)
            summed, top, total = attend_own(h)
            own_sum[h] = summed
            own_top[h] = jnp.broadcast_to(top, (rows, HD))
            own_total[h] = jnp.broadcast_to(total, (rows, HD))
        cross()
        for h in range(heads):
            for t in range(2):
                o_copy(h, t).wait_recv()
            level = jnp.transpose(jnp.broadcast_to(l_in[h, 0:1], (HD, rows)))
            top = own_top[h]
            peak = jnp.maximum(top, level)
            own, far = jnp.exp2(top - peak), jnp.exp2(level - peak)
            summed = own_sum[h] * own + o_in[:, cols(h)].astype(jnp.float32) * far
            so_ref[:, cols(h)] = (summed / (own_total[h] * own + far)).astype(so_ref.dtype)
        for h in range(heads):
            q_copy(h).wait_send()

    for h in range(heads):
        for d in range(1, half):
            for t in range(2):
                kv_copy(d, h, t).wait_send()
    for d in range(1, group):
        nb_copy(d).wait_send()


def on_device(sizes, query_self, key_self, value_self, query_cross, neighbour_kv, neighbour_map):
    rows, width = query_self.shape
    heads = width // HD
    half = sizes[1] // 2
    group = sizes[0] * sizes[2]
    slots, block_len, _ = neighbour_kv.shape
    bf16, f32 = jnp.bfloat16, jnp.float32
    vmem = pl.BlockSpec(memory_space=pltpu.VMEM)
    out = jax.ShapeDtypeStruct((rows, width), bf16)
    pairs = rows * rows * heads * (2 * half)
    return pl.pallas_call(
        functools.partial(kernel, sizes),
        out_shape=(out, out),
        in_specs=[pl.BlockSpec(memory_space=pltpu.SMEM)]
        + [vmem] * 4
        + [pl.BlockSpec(memory_space=pl.ANY)],
        out_specs=(vmem, vmem),
        scratch_shapes=[
            pltpu.VMEM((half, rows, width), bf16),
            pltpu.VMEM((half, rows, width), bf16),
            pltpu.VMEM((rows, width), bf16),
            pltpu.VMEM((rows, width), bf16),
            pltpu.VMEM((heads, 8, rows), f32),
            pltpu.VMEM((rows, width), bf16),
            pltpu.VMEM((heads, 8, rows), f32),
            pltpu.VMEM((heads, rows, HD), f32),
            pltpu.VMEM((heads, rows, HD), f32),
            pltpu.VMEM((heads, rows, HD), f32),
            pltpu.VMEM((group * slots, block_len, 2 * width), bf16),
            pltpu.SemaphoreType.DMA((half - 1, heads, 2)),
            pltpu.SemaphoreType.DMA((half - 1, heads, 2)),
            pltpu.SemaphoreType.DMA((heads,)),
            pltpu.SemaphoreType.DMA((heads,)),
            pltpu.SemaphoreType.DMA((heads, 2)),
            pltpu.SemaphoreType.DMA((heads, 2)),
            pltpu.SemaphoreType.DMA((group - 1,)),
            pltpu.SemaphoreType.DMA((group - 1,)),
            pltpu.SemaphoreType.DMA,
        ],
        compiler_params=pltpu.CompilerParams(
            collective_id=0, has_side_effects=True, vmem_limit_bytes=56 * 1024 * 1024
        ),
        cost_estimate=pl.CostEstimate(
            flops=4 * pairs * HD, bytes_accessed=2 * 1024 * 1024, transcendentals=pairs
        ),
    )(neighbour_map, query_self, key_self, value_self, query_cross, neighbour_kv)


def solution(mesh):
    sizes = tuple(mesh.shape[a] for a in ("sec", "ctx", "head"))
    split = P("ctx", ("sec", "head"))
    return jax.shard_map(
        functools.partial(on_device, sizes),
        mesh=mesh,
        in_specs=(split, split, split, split, P(("sec", "ctx", "head"), None, None), P("ctx", None)),
        out_specs=(split, split),
        check_vma=False,
    )
```

time: 120 us -> 37.7 us (0.31)
  the two profiles are of different devices: /device:TPU:25 before, /device:TPU:0 now
where the time goes in v1:
time: 37.7 us; the launch traced here: 37.6 us
  Pallas kernels  33.2 us (88%)
  local copies, waits for them, and re-layouts  3.67 us (10%)
  between operations  0.65 us (2%)
    pallas_call x1, Pallas kernels, on_device(): pl.pallas_call(functools.partial(kernel, sizes), out_shape=(out, out), in...  33.2 us
    unnamed x5, local copies, waits for them, and re-layouts  3.67 us

profile of v1, /device:TPU:0, one launch (start us, length us, event | category | flops | bytes accessed | tf_op | source)
XLA Modules:
  0.0 37.6 jit_solution(14755364002824500497)
XLA Ops:
  0.6 1.3 %copy.8.map_ref = s32[3,2]{1,0:T(4,128)} copy(s32[3,2]{0,1:T(2,128)} %param.11) | data formatting | bytes 48 | tf_op args[5]
  2.0 33.2 %shard_map.77 = (bf16[192,512]{1,0:T(8,128)(2,1)}, bf16[192,512]{1,0:T(8,128)(2,1)}) custom-call(s32[3,2]{1,0:T(4,128)} %copy.8.map_ref, bf16[192,512]{1,0:T(8,128)(2,1)} %qs_ref.1, bf16[192,512]{1,0:T(8,128)(2,1)} %k_ref.1, bf16[192,512]{1,0:T(8,128)(2,1)} %v_ref.1, bf16[192,512]{1,0:T(8,128)(2,1)} %qc_ref.1, bf16[1,128,4096]{2,1,0:T(8,128)(2,1)} %nb_ref.1), custom_call_target="tpu_custom_call" | custom-call | flops 603979776 | bytes 2097152 | tf_op jit(solution)/shard_map/pallas_call | solution.py:247
  35.2 0.0 copy-start
  35.2 1.7 %copy.11 = bf16[192,512]{1,0:T(8,128)(2,1)} copy(bf16[192,512]{1,0:T(8,128)(2,1)} %get-tuple-element.4) | data formatting | bytes 393216
  36.9 0.0 copy-done
  36.9 0.7 %copy.12 = bf16[192,512]{1,0:T(8,128)(2,1)} copy(bf16[192,512]{1,0:T(8,128)(2,1)S(1)} %copy-done) | data formatting | bytes 393216
Async XLA Ops:
  35.2 1.7 %copy-start = (bf16[192,512]{1,0:T(8,128)(2,1)S(1)}, bf16[192,512]{1,0:T(8,128)(2,1)}, u32[]{:S(2)}) copy-start(bf16[192,512]{1,0:T(8,128)(2,1)} %get-tuple-element.5) | copy-start | bytes 589828

commit v2 on v1

--- a/solution.py
+++ b/solution.py
@@ -11,6 +11,7 @@
 HD = 128
 STRETCH = 64
 MASKED_SCORE = -1e30
+AHEAD = 2
 MESH = pl.DeviceIdType.MESH
 BASE2 = math.log2(math.e) / math.sqrt(HD)
 
@@ -35,11 +36,15 @@
 def kernel(
     sizes,
     map_ref,
-    qs_ref,
+    qs_hbm,
     k_ref,
     v_ref,
+    qc_hbm,
+    nb_ref,
+    so_hbm,
+    co_hbm,
+    qs_ref,
     qc_ref,
-    nb_ref,
     so_ref,
     co_ref,
     k_all,
@@ -61,7 +66,8 @@
     o_recv,
     nb_send,
     nb_recv,
-    nb_own,
+    load,
+    store,
 ):
     n_sec, n_ctx, n_head = sizes
     half = n_ctx // 2
@@ -81,8 +87,20 @@
         other = lax.rem(within + d, group)
         return other, {"sec": other // n_head, "head": lax.rem(other, n_head)}
 
+    def flipped(d):
+        place, bit = mine, 1
+        while bit <= d:
+            if d & bit:
+                place = place + bit - 2 * bit * lax.rem(place // bit, 2)
+            bit *= 2
+        return place
+
+    def last_bit(d, h, t):
+        bits = [1 << i for i in range(d.bit_length()) if d >> i & 1]
+        return bits[-1] if t == 1 and h % 2 == 1 else bits[0]
+
     def peer(d):
-        return base + lax.rem(mine + d, half)
+        return base + flipped(d)
 
     def cols(h):
         return slice(h * HD, (h + 1) * HD)
@@ -93,11 +111,30 @@
     pl.semaphore_signal(barrier, inc=1, device_id={"ctx": partner}, device_id_type=MESH)
     for d in range(1, group):
         pl.semaphore_signal(barrier, inc=1, device_id=member(d)[1], device_id_type=MESH)
+
+    own_start = pl.multiple_of(within * (2 * width), 2 * width)
+    loads = [
+        pltpu.make_async_copy(source, target, load.at[i])
+        for i, (source, target) in enumerate(
+            (
+                (qs_hbm, qs_ref),
+                (k_ref, k_all.at[mine]),
+                (v_ref, v_all.at[mine]),
+                (qc_hbm, qc_ref),
+                (
+                    nb_ref.at[:, :, pl.ds(own_start, 2 * width)],
+                    nb_all.at[pl.ds(within * slots, slots)],
+                ),
+            )
+        )
+    ]
+    for copy in loads:
+        copy.start()
     pl.semaphore_wait(barrier, half - 1 + 1 + group - 1)
 
     def q_copy(h):
         return pltpu.make_async_remote_copy(
-            src_ref=qs_ref.at[:, cols(h)],
+            src_ref=qs_hbm.at[:, cols(h)],
             dst_ref=q_in.at[:, cols(h)],
             send_sem=q_send.at[h],
             recv_sem=q_recv.at[h],
@@ -106,13 +143,16 @@
         )
 
     def kv_copy(d, h, t):
-        source, gathered = ((k_ref, k_all), (v_ref, v_all))[t]
+        own, gathered = ((k_ref, k_all), (v_ref, v_all))[t]
+        bit = last_bit(d, h, t)
+        origin = flipped(d - bit)
+        source = own if d == bit else gathered.at[origin]
         return pltpu.make_async_remote_copy(
             src_ref=source.at[:, cols(h)],
-            dst_ref=gathered.at[mine, :, cols(h)],
+            dst_ref=gathered.at[origin, :, cols(h)],
             send_sem=kv_send.at[d - 1, h, t],
             recv_sem=kv_recv.at[d - 1, h, t],
-            device_id={"ctx": peer(d)},
+            device_id={"ctx": peer(bit)},
             device_id_type=MESH,
         )
 
@@ -139,32 +179,40 @@
             device_id_type=MESH,
         )
 
-    for h in range(heads):
-        pl.when(upper)(lambda h=h: q_copy(h).start())
-        for d in range(1, half):
-            for t in range(2):
-                kv_copy(d, h, t).start()
+    offsets = sorted(range(1, half), key=lambda d: (d.bit_count(), d))
+    arrived = set()
+
+    def wait_kv(d, h, t):
+        if (d, h, t) not in arrived:
+            arrived.add((d, h, t))
+            kv_copy(d, h, t).wait_recv()
+
+    def send_own(h):
+        pl.when(upper)(lambda: q_copy(h).start())
+        for d in offsets:
+            if d.bit_count() == 1:
+                for t in range(2):
+                    kv_copy(d, h, t).start()
+
+    def send_on(h):
+        for d in offsets:
+            if d.bit_count() > 1:
+                for t in range(2):
+                    wait_kv(d - last_bit(d, h, t), h, t)
+                    kv_copy(d, h, t).start()
+
+    for h in range(min(AHEAD, heads)):
+        send_own(h)
         if h == 0:
             for d in range(1, group):
                 nb_copy(d).start()
-    own_nb = pltpu.make_async_copy(
-        nb_ref.at[:, :, pl.ds(pl.multiple_of(within * (2 * width), 2 * width), 2 * width)],
-        nb_all.at[pl.ds(within * slots, slots)],
-        nb_own,
-    )
-    own_nb.start()
-    k_all[mine] = k_ref[...]
-    v_all[mine] = v_ref[...]
+    for copy in loads[:3]:
+        copy.wait()
 
     def gathered_head(h):
         keys = k_all[:, :, cols(h)].reshape(half * rows, HD)
         values = v_all[:, :, cols(h)].reshape(half * rows, HD)
         return keys, values
-
-    def wait_kv(h):
-        for d in range(1, half):
-            for t in range(2):
-                kv_copy(d, h, t).wait_recv()
 
     def attend_own(h):
         keys, values = gathered_head(h)
@@ -173,11 +221,12 @@
         return attend(qs_ref[:, cols(h)], keys, values, place <= position)
 
     def cross():
-        own_nb.wait()
+        for copy in loads[3:]:
+            copy.wait()
         for d in range(1, group):
             nb_copy(d).wait_recv()
         for c in range(rows // STRETCH):
-            picks = [map_ref[c, r] for r in range(map_ref.shape[1])]
+            picks = [map_ref[r, c] for r in range(map_ref.shape[0])]
             part = slice(c * STRETCH, (c + 1) * STRETCH)
             keep = jnp.logical_or(ctx > 0, c > 0)
             for h in range(heads):
@@ -186,52 +235,72 @@
                 summed, _, total = attend(qc_ref[part, cols(h)], keys, values)
                 co_ref[part, cols(h)] = jnp.where(keep, summed / total, 0.0).astype(co_ref.dtype)
 
-    @pl.when(jnp.logical_not(upper))
+    def serve(h):
+        q_copy(h).wait_recv()
+        keys, values = gathered_head(h)
+        summed, top, total = attend(q_in[:, cols(h)], keys, values)
+        o_part[:, cols(h)] = (summed / total).astype(o_part.dtype)
+        level = jnp.broadcast_to(top + jnp.log2(total), (rows, HD))
+        l_part[h] = jnp.transpose(level)[:8]
+        for t in range(2):
+            o_copy(h, t).start()
+
+    def keep(h):
+        summed, top, total = attend_own(h)
+        own_sum[h] = summed
+        own_top[h] = jnp.broadcast_to(top, (rows, HD))
+        own_total[h] = jnp.broadcast_to(total, (rows, HD))
+
+    def finish(h):
+        summed, _, total = attend_own(h)
+        so_ref[:, cols(h)] = (summed / total).astype(so_ref.dtype)
+
+    def merge(h):
+        for t in range(2):
+            o_copy(h, t).wait_recv()
+        level = jnp.transpose(jnp.broadcast_to(l_in[h, 0:1], (HD, rows)))
+        top = own_top[h]
+        peak = jnp.maximum(top, level)
+        own, far = jnp.exp2(top - peak), jnp.exp2(level - peak)
+        summed = own_sum[h] * own + o_in[:, cols(h)].astype(jnp.float32) * far
+        so_ref[:, cols(h)] = (summed / (own_total[h] * own + far)).astype(so_ref.dtype)
+
+    lower = jnp.logical_not(upper)
+    for h in range(heads):
+        if h == heads - 1:
+            cross()
+            pltpu.make_async_copy(co_ref, co_hbm, store.at[1]).start()
+        for later in (range(min(2, heads)) if h == 0 else range(h + 1, min(h + 2, heads))):
+            send_on(later)
+            if later + AHEAD < heads:
+                send_own(later + AHEAD)
+        for d in offsets:
+            for t in range(2):
+                wait_kv(d, h, t)
+        pl.when(lower)(lambda: serve(h))
+        pl.when(lower)(lambda: finish(h))
+        pl.when(upper)(lambda: keep(h))
+    @pl.when(upper)
     def _():
         for h in range(heads):
-            wait_kv(h)
-            q_copy(h).wait_recv()
-            keys, values = gathered_head(h)
-            summed, top, total = attend(q_in[:, cols(h)], keys, values)
-            o_part[:, cols(h)] = (summed / total).astype(o_part.dtype)
-            level = jnp.broadcast_to(top + jnp.log2(total), (rows, HD))
-            l_part[h] = jnp.transpose(level)[:8]
-            for t in range(2):
-                o_copy(h, t).start()
-            summed, _, total = attend_own(h)
-            so_ref[:, cols(h)] = (summed / total).astype(so_ref.dtype)
-        cross()
+            merge(h)
+            q_copy(h).wait_send()
+
+    @pl.when(lower)
+    def _():
         for h in range(heads):
             for t in range(2):
                 o_copy(h, t).wait_send()
 
-    @pl.when(upper)
-    def _():
-        for h in range(heads):
-            wait_kv(h)
-            summed, top, total = attend_own(h)
-            own_sum[h] = summed
-            own_top[h] = jnp.broadcast_to(top, (rows, HD))
-            own_total[h] = jnp.broadcast_to(total, (rows, HD))
-        cross()
-        for h in range(heads):
-            for t in range(2):
-                o_copy(h, t).wait_recv()
-            level = jnp.transpose(jnp.broadcast_to(l_in[h, 0:1], (HD, rows)))
-            top = own_top[h]
-            peak = jnp.maximum(top, level)
-            own, far = jnp.exp2(top - peak), jnp.exp2(level - peak)
-            summed = own_sum[h] * own + o_in[:, cols(h)].astype(jnp.float32) * far
-            so_ref[:, cols(h)] = (summed / (own_total[h] * own + far)).astype(so_ref.dtype)
-        for h in range(heads):
-            q_copy(h).wait_send()
-
+    pltpu.make_async_copy(so_ref, so_hbm, store.at[0]).start()
     for h in range(heads):
         for d in range(1, half):
             for t in range(2):
                 kv_copy(d, h, t).wait_send()
     for d in range(1, group):
         nb_copy(d).wait_send()
+    pltpu.make_async_copy(so_ref, so_hbm, store.at[0]).wait()
+    pltpu.make_async_copy(co_ref, co_hbm, store.at[1]).wait()
 
 
 def on_device(sizes, query_self, key_self, value_self, query_cross, neighbour_kv, neighbour_map):
@@ -241,17 +310,20 @@
     group = sizes[0] * sizes[2]
     slots, block_len, _ = neighbour_kv.shape
     bf16, f32 = jnp.bfloat16, jnp.float32
-    vmem = pl.BlockSpec(memory_space=pltpu.VMEM)
+    anywhere = pl.BlockSpec(memory_space=pl.ANY)
     out = jax.ShapeDtypeStruct((rows, width), bf16)
     pairs = rows * rows * heads * (2 * half)
     return pl.pallas_call(
         functools.partial(kernel, sizes),
         out_shape=(out, out),
         in_specs=[pl.BlockSpec(memory_space=pltpu.SMEM)]
-        + [vmem] * 4
-        + [pl.BlockSpec(memory_space=pl.ANY)],
-        out_specs=(vmem, vmem),
+        + [anywhere] * 5,
+        out_specs=(anywhere, anywhere),
         scratch_shapes=[
+            pltpu.VMEM((rows, width), bf16),
+            pltpu.VMEM((rows, width), bf16),
+            pltpu.VMEM((rows, width), bf16),
+            pltpu.VMEM((rows, width), bf16),
             pltpu.VMEM((half, rows, width), bf16),
             pltpu.VMEM((half, rows, width), bf16),
             pltpu.VMEM((rows, width), bf16),
@@ -271,7 +343,8 @@
             pltpu.SemaphoreType.DMA((heads, 2)),
             pltpu.SemaphoreType.DMA((group - 1,)),
             pltpu.SemaphoreType.DMA((group - 1,)),
-            pltpu.SemaphoreType.DMA,
+            pltpu.SemaphoreType.DMA((5,)),
+            pltpu.SemaphoreType.DMA((2,)),
         ],
         compiler_params=pltpu.CompilerParams(
             collective_id=0, has_side_effects=True, vmem_limit_bytes=56 * 1024 * 1024
@@ -279,7 +352,7 @@
         cost_estimate=pl.CostEstimate(
             flops=4 * pairs * HD, bytes_accessed=2 * 1024 * 1024, transcendentals=pairs
         ),
-    )(neighbour_map, query_self, key_self, value_self, query_cross, neighbour_kv)
+    )(jnp.transpose(neighbour_map), query_self, key_self, value_self, query_cross, neighbour_kv)
 
 
 def solution(mesh):

time: 37.7 us -> 33 us (0.88)
  Pallas kernels: 33.2 us -> 29.9 us
  local copies, waits for them, and re-layouts: 3.67 us -> 2.34 us
    pallas_call x1, Pallas kernels: 33.2 us -> 29.9 us  [on_device(): pl.pallas_call(functools.partial(kernel, sizes), out_shape=(out, out), in...]
    unnamed x5 -> x4, local copies, waits for them, and re-layouts: 3.67 us -> 2.34 us
where the time goes in v2:
time: 33 us; the launch traced here: 32.8 us
  Pallas kernels  29.9 us (91%)
  local copies, waits for them, and re-layouts  2.34 us (7%)
  between operations  0.65 us (2%)
    pallas_call x1, Pallas kernels, on_device(): pl.pallas_call(functools.partial(kernel, sizes), out_shape=(out, out), in...  29.9 us
    unnamed x4, local copies, waits for them, and re-layouts  2.34 us

profile of v2, /device:TPU:0, one launch (start us, length us, event | category | flops | bytes accessed | tf_op | source)
XLA Modules:
  0.0 32.8 jit_solution(4992412330316604125)
XLA Ops:
  0.6 29.9 %shard_map.77 = (bf16[192,512]{1,0:T(8,128)(2,1)}, bf16[192,512]{1,0:T(8,128)(2,1)}) custom-call(s32[2,3]{1,0:T(2,128)} %bitcast.1, bf16[192,512]{1,0:T(8,128)(2,1)} %qs_hbm.1, bf16[192,512]{1,0:T(8,128)(2,1)} %k_ref.1, bf16[192,512]{1,0:T(8,128)(2,1)} %v_ref.1, bf16[192,512]{1,0:T(8,128)(2,1)} %qc_hbm.1, bf16[1,128,4096]{2,1,0:T(8,128)(2,1)} %nb_ref.1), custom_call_target="tpu_custom_call" | custom-call | flops 603979776 | bytes 2097152 | tf_op jit(solution)/shard_map/pallas_call | solution.py:316
  30.5 0.0 copy-start
  30.5 1.7 %copy.10 = bf16[192,512]{1,0:T(8,128)(2,1)} copy(bf16[192,512]{1,0:T(8,128)(2,1)} %get-tuple-element.4) | data formatting | bytes 393216
  32.2 0.0 copy-done
  32.2 0.7 %copy.11 = bf16[192,512]{1,0:T(8,128)(2,1)} copy(bf16[192,512]{1,0:T(8,128)(2,1)S(1)} %copy-done) | data formatting | bytes 393216
Async XLA Ops:
  30.5 1.7 %copy-start = (bf16[192,512]{1,0:T(8,128)(2,1)S(1)}, bf16[192,512]{1,0:T(8,128)(2,1)}, u32[]{:S(2)}) copy-start(bf16[192,512]{1,0:T(8,128)(2,1)} %get-tuple-element.5) | copy-start | bytes 589828
